TPU v7x, 32 devices: a whole 2x2x4 slice. The times are simulated.
32 devices in a mesh: grp: 4 (over z), seq: 8 (over y, x, core).
Axes of the slice: x: 2, y: 2, z: 4, core: 2. Of those that a mesh axis runs over, the one named last changes fastest.
Arguments:
- main_query: bfloat16 [8, 128, 2560], P('seq', 'grp'), may hold values from -150 to 150
- main_key: bfloat16 [8, 128, 2560], P('seq', 'grp'), may hold values from -4 to 4
- main_value: bfloat16 [8, 128, 2560], P('seq', 'grp'), may hold values from -240 to 240
- guide_query: bfloat16 [8, 128, 1024], P('seq', None, 'grp'), may hold values from -150 to 150
- guide_key: bfloat16 [8, 128, 1024], P('seq', None, 'grp'), may hold values from -4 to 4
- guide_value: bfloat16 [8, 128, 1024], P('seq', None, 'grp'), may hold values from -240 to 240
- latents: float32 [8, 128, 64], P('seq', 'grp'), may hold values from -6 to 6
- step_index: int32 [1], replicated, may hold values from 0 to 49
- main_mod: bfloat16 [50, 2, 2560], replicated, may hold values from -3 to 3
- guide_mod: bfloat16 [50, 2, 1024], replicated, may hold values from -3 to 3
- main_head: bfloat16 [2560, 64], replicated, may hold values from -0.125 to 0.125
- guide_head: bfloat16 [1024, 64], replicated, may hold values from -0.1875 to 0.1875
Outputs:
- velocity: float32 [8, 128, 64], P('seq', 'grp')
- next_latents: float32 [8, 128, 64], P('seq', 'grp')
All inputs are finite; a program needn't handle non-finite values.
Results may differ from a plain program's by a relative error of at most 0.012.
Values may be sent and summed in bfloat16 or wider, within the bound.
A program may use at most 128 MiB of HBM per device.

v0:
```python
import math

import jax
import jax.numpy as jnp
from jax import lax
from jax.sharding import PartitionSpec as P

HD = 128
STEPS = 50


guidance = 2.5
flow_shift = 3.0
epsilon = 1e-06
very_low = -1e30


def sigma_at(index):
    remaining = 1.0 - index.astype(jnp.float32) / STEPS
    return flow_shift * remaining / (1.0 + (flow_shift - 1.0) * remaining)


def fresh_state(queries):
    rows, heads, depth = queries.shape
    return (
        jnp.full((heads, rows), very_low, jnp.float32),
        jnp.zeros((heads, rows), jnp.float32),
        jnp.zeros((rows, heads, depth), jnp.float32),
    )


def fold_keys(carried, queries, keys, values):
    rows, heads, depth = queries.shape
    length = keys.shape[1]
    block = math.gcd(length, 512)
    key_blocks = keys.reshape(length // block, block, heads, depth)
    value_blocks = values.reshape(length // block, block, heads, depth)
    factor = 1.0 / math.sqrt(depth)

    def one_block(running, blocks):
        highest, weight_sum, numerator = running
        key_block, value_block = blocks
        scores = (
            jnp.einsum("rhd,bhd->hrb", queries, key_block, preferred_element_type=jnp.float32)
            * factor
        )
        raised = jnp.maximum(highest, jnp.max(scores, axis=-1))
        shrink = jnp.exp(highest - raised)
        weights = jnp.exp(scores - raised[:, :, None])
        weight_sum = weight_sum * shrink + jnp.sum(weights, axis=-1)
        numerator = numerator * jnp.transpose(shrink)[:, :, None] + jnp.einsum(
            "hrb,bhd->rhd",
            weights.astype(jnp.bfloat16),
            value_block,
            preferred_element_type=jnp.float32,
        )
        return ((raised, weight_sum, numerator), None)

    carried, unused = lax.scan(one_block, carried, (key_blocks, value_blocks))
    return carried


def finish_state(carried):
    highest, weight_sum, numerator = carried
    rows, heads, depth = numerator.shape
    result = numerator / jnp.transpose(weight_sum)[:, :, None]
    return lax.optimization_barrier(result.reshape(rows, heads * depth).astype(jnp.bfloat16))


def table_row(table, step_now):
    return lax.dynamic_index_in_dim(table, step_now, 0, keepdims=False).astype(jnp.float32)


def project_whole(attended, table, step_now, weight):
    row_now = table_row(table, step_now)
    values = attended.astype(jnp.float32)
    center = jnp.mean(values, axis=-1, keepdims=True)
    centered = values - center
    spread = jnp.mean(centered * centered, axis=-1, keepdims=True)
    normed = centered * lax.rsqrt(spread + epsilon)
    modulated = normed * (1.0 + row_now[1]) + row_now[0]
    return jnp.dot(modulated, weight.astype(jnp.float32), precision=lax.Precision.HIGHEST)


def on_device(
    main_query,
    main_key,
    main_value,
    guide_query,
    guide_key,
    guide_value,
    latents,
    step_index,
    main_mod,
    guide_mod,
    main_head,
    guide_head,
):
    step_now = step_index[0]
    moved_query, moved_key, moved_value = (
        lax.all_to_all(main_query, "grp", split_axis=2, concat_axis=1, tiled=True),
        lax.all_to_all(main_key, "grp", split_axis=2, concat_axis=1, tiled=True),
        lax.all_to_all(main_value, "grp", split_axis=2, concat_axis=1, tiled=True),
    )
    rows = moved_query.shape[1]
    main_queries = moved_query[0].reshape(rows, moved_query.shape[2] // HD, HD)
    guide_queries = guide_query[0].reshape(rows, guide_query.shape[2] // HD, HD)
    pieces = (
        lax.all_gather(moved_key, "seq", axis=1, tiled=True),
        lax.all_gather(moved_value, "seq", axis=1, tiled=True),
    )
    main_state = fold_keys(fresh_state(main_queries), main_queries, pieces[0], pieces[1])
    pieces = (
        lax.all_gather(guide_key, "seq", axis=1, tiled=True),
        lax.all_gather(guide_value, "seq", axis=1, tiled=True),
    )
    guide_state = fold_keys(fresh_state(guide_queries), guide_queries, pieces[0], pieces[1])
    main_out = finish_state(main_state)
    guide_out = finish_state(guide_state)
    main_back, guide_back = (
        lax.all_to_all(main_out[None], "grp", split_axis=1, concat_axis=2, tiled=True),
        lax.all_to_all(guide_out[None], "grp", split_axis=1, concat_axis=2, tiled=True),
    )
    main_flow = project_whole(main_back[0], main_mod, step_now, main_head)[None]
    guide_flow = project_whole(guide_back[0], guide_mod, step_now, guide_head)[None]
    velocity = guide_flow + guidance * (main_flow - guide_flow)
    advanced = latents + (sigma_at(step_now + 1) - sigma_at(step_now)) * velocity
    return (velocity, advanced)


def solution(mesh):
    return jax.shard_map(
        on_device,
        mesh=mesh,
        in_specs=(
            P("seq", "grp", None),
            P("seq", "grp", None),
            P("seq", "grp", None),
            P("seq", None, "grp"),
            P("seq", None, "grp"),
            P("seq", None, "grp"),
            P("seq", "grp", None),
            P(),
            P(),
            P(),
            P(),
            P(),
        ),
        out_specs=(P("seq", "grp", None), P("seq", "grp", None)),
        check_vma=False,
    )
```

profile of v0, /device:TPU:0, one launch (start us, length us, event | category | flops | bytes accessed | tf_op | source)
XLA Modules:
  0.0 163.6 jit_solution(7764050422387910480)
XLA Ops:
  7.2 2.3 %copy.85 = bf16[1,32,2560]{1,0,2:T(2,128)(2,1)S(1)} copy(bf16[1,32,2560]{2,1,0:T(8,128)(2,1)} %param.17) | data formatting | bytes 327680 | tf_op args[1]
  9.5 0.5 broadcast.157
  10.0 14.3 %reduce.17 = bf16[2560,32]{1,0:T(8,128)(2,1)S(1)} reduce(bf16[2560,1,32]{2,1,0:T(2,128)(2,1)S(1)} %bitcast.105, bf16[]{:T(256)} %broadcast.157), dimensions={1}, to_apply=%bitcast.62.reduce_sub_computation | reduce | bytes 327682
  24.3 0.6 reshape.111
  24.9 13.1 %all_to_all.69 = bf16[4,2,10240]{2,1,0:T(2,128)(2,1)S(1)} all-to-all(bf16[4,2,10240]{2,1,0:T(2,128)(2,1)S(1)} %reshape.111), channel_id=1, replica_groups=mesh['grp'=4,'seq'=8] {'grp'}, dimensions={0} | all-to-all | bytes 327680 | tf_op jit(solution)/shard_map/all_to_all | solution.py:102
  38.0 0.8 reshape.112
  38.8 0.7 copy.86
  39.5 0.7 copy.87
  40.2 0.9 copy.92
  41.2 14.3 %reduce.19 = bf16[2560,32]{1,0:T(8,128)(2,1)S(1)} reduce(bf16[2560,1,32]{2,1,0:T(2,128)(2,1)S(1)} %bitcast.109, bf16[]{:T(256)} %broadcast.157), dimensions={1}, to_apply=%bitcast.66.reduce_sub_computation | reduce | bytes 327682
  55.5 1.3 reshape.115
  56.8 3.3 %all-to-all-start.3 = ((bf16[4,2,10240]{2,1,0:T(2,128)(2,1)}), bf16[4,2,10240]{2,1,0:T(2,128)(2,1)S(1)}, u32[]{:S(2)}, u32[]{:S(2)}) async-start(bf16[4,2,10240]{2,1,0:T(2,128)(2,1)} %reshape.115), calls=%async_computation.3 | async-start | bytes 327680 | tf_op jit(solution)/shard_map/all_to_all | solution.py:103
  60.2 10.0 %all_gather.12 = bf16[1,1024,256]{2,1,0:T(8,128)(2,1)S(1)} all-gather(bf16[1,128,256]{2,1,0:T(8,128)(2,1)S(1)} %copy-done.6), channel_id=1, replica_groups=mesh['grp'=4,'seq'=8] {'seq'}, dimensions={1}, use_global_device_ids=true | all-gather | bytes 589824 | tf_op jit(solution)/shard_map/all_gather | solution.py:114
  70.4 9.8 %all_gather.13 = bf16[1,1024,256]{2,1,0:T(8,128)(2,1)S(1)} all-gather(bf16[1,128,256]{2,1,0:T(8,128)(2,1)S(1)} %copy-done.7), channel_id=1, replica_groups=mesh['grp'=4,'seq'=8] {'seq'}, dimensions={1}, use_global_device_ids=true | all-gather | bytes 589824 | tf_op jit(solution)/shard_map/all_gather | solution.py:115
  80.7 0.8 reshape.116
  81.5 0.7 copy.93
  82.2 0.7 copy.94
  83.0 2.4 %while.30 = (s32[]{:T(128)}, f32[2,128]{1,0:T(2,128)S(1)}, f32[2,128]{1,0:T(2,128)S(1)}, f32[128,2,128]{0,2,1:T(8,128)S(1)}, bf16[2,512,2,128]{3,2,1,0:T(2,128)(...) while((s32[]{:T(128)}, f32[2,128]{1,0:T(2,128)S(1)}, ...), condition=%wide.region_3.4_spmd.clone, body=%wide.region_0.3_spmd.clone.sunk | while | flops 67995136 | bytes 4014189 | solution.py:59
  83.0 0.4 constant_dynamic-slice_fusion.3
  84.2 0.4 constant_dynamic-slice_fusion.3
  85.6 1.0 reduce.16
  86.7 0.6 reshape.109
  87.3 5.0 %all-to-all-start = ((bf16[4,2,4096]{2,1,0:T(2,128)(2,1)}), bf16[4,2,4096]{2,1,0:T(2,128)(2,1)S(1)}, u32[]{:S(2)}, u32[]{:S(2)}) async-start(bf16[4,2,4096]{2,1,0:T(2,128)(2,1)} %reshape.109), calls=%async_computation | async-start | bytes 131072 | tf_op jit(solution)/shard_map/all_to_all | solution.py:122
  93.0 0.9 copy.89
  93.9 14.3 %reduce.18 = bf16[2560,32]{1,0:T(8,128)(2,1)S(1)} reduce(bf16[2560,1,32]{2,1,0:T(2,128)(2,1)S(1)} %bitcast.110, bf16[]{:T(256)} %broadcast.157), dimensions={1}, to_apply=%bitcast.64.reduce_sub_computation | reduce | bytes 327682
  108.2 1.3 reshape.113
  109.6 0.7 dynamic-slice_convert_fusion.1
  110.3 0.7 dynamic-slice_convert_fusion
  111.0 5.1 %all-to-all-start.2 = ((bf16[4,2,10240]{2,1,0:T(2,128)(2,1)}), bf16[4,2,10240]{2,1,0:T(2,128)(2,1)S(1)}, u32[]{:S(2)}, u32[]{:S(2)}) async-start(bf16[4,2,10240]{2,1,0:T(2,128)(2,1)} %reshape.113), calls=%async_computation.2 | async-start | bytes 327680 | tf_op jit(solution)/shard_map/all_to_all | solution.py:101
  116.5 0.6 copy-done.1
  117.3 5.3 %all-to-all-done.2 = bf16[4,2,10240]{2,1,0:T(2,128)(2,1)S(1)} async-done(((bf16[4,2,10240]{2,1,0:T(2,128)(2,1)}), bf16[4,2,10240]{2,1,0:T(2,128)(2,1)S(1)}, u32[]{:S(2)}, u32[]{:S(2)}) %all-to-all-start.2) | async-done | bytes 163872 | tf_op jit(solution)/shard_map/all_to_all | solution.py:101
  122.6 0.8 reshape.114
  123.4 0.7 copy.90
  124.4 4.1 %reshape.105 = bf16[2,512,5,128]{3,2,1,0:T(8,128)(2,1)} reshape(bf16[1,1024,640]{2,1,0:T(8,128)(2,1)} %all-gather.3.cloned.1.call-done) | data formatting | bytes 2621440 | tf_op jit(solution)/shard_map/reshape | solution.py:36
  128.6 1.8 %copy.96 = bf16[2,512,5,128]{3,1,2,0:T(8,128)(2,1)S(1)} copy(bf16[2,512,5,128]{3,2,1,0:T(8,128)(2,1)} %reshape.105) | data formatting | bytes 2621440
  130.4 4.1 %reshape.106 = bf16[2,512,5,128]{3,2,1,0:T(8,128)(2,1)} reshape(bf16[1,1024,640]{2,1,0:T(8,128)(2,1)} %all-gather.5.cloned.1.call-done) | data formatting | bytes 2621440 | tf_op jit(solution)/shard_map/reshape | solution.py:37
  134.5 4.1 %copy.98 = bf16[2,512,5,128]{1,3,2,0:T(8,128)(2,1)} copy(bf16[2,512,5,128]{3,2,1,0:T(8,128)(2,1)} %reshape.106) | data formatting | bytes 2621440
  138.6 4.1 %while.31 = (s32[]{:T(128)}, f32[5,128]{1,0:T(8,128)S(1)}, f32[5,128]{1,0:T(8,128)S(1)}, f32[128,5,128]{0,2,1:T(8,128)S(1)}, bf16[2,512,5,128]{3,1,2,0:T(8,128)(...) while((s32[]{:T(128)}, f32[5,128]{1,0:T(8,128)S(1)}, ...), condition=%wide.region_10.11_spmd.clone, body=%wide.region_7.0_spmd.clone.sunk | while | flops 169987840 | bytes 6103661 | solution.py:59
  138.6 0.3 fusion.80
  139.0 1.5 fusion.84
  140.7 0.3 fusion.80
  141.1 1.5 fusion.84
  143.1 1.6 reduce.20
  144.7 0.7 reshape.117
  145.4 3.3 %all-to-all-start.4 = ((bf16[4,2,10240]{2,1,0:T(2,128)(2,1)}), bf16[4,2,10240]{2,1,0:T(2,128)(2,1)S(1)}, u32[]{:S(2)}, u32[]{:S(2)}) async-start(bf16[4,2,10240]{2,1,0:T(2,128)(2,1)} %reshape.117), calls=%async_computation.4 | async-start | bytes 327680 | tf_op jit(solution)/shard_map/all_to_all | solution.py:121
  148.9 0.3 fusion.34
  149.2 5.5 %all-to-all-done.4 = bf16[4,2,10240]{2,1,0:T(2,128)(2,1)S(1)} async-done(((bf16[4,2,10240]{2,1,0:T(2,128)(2,1)}), bf16[4,2,10240]{2,1,0:T(2,128)(2,1)S(1)}, u32[]{:S(2)}, u32[]{:S(2)}) %all-to-all-start.4) | async-done | bytes 163872 | tf_op jit(solution)/shard_map/all_to_all | solution.py:121
  155.7 1.1 bitcast_add_fusion
  (92 shorter events, 5.1 us)
Async XLA Ops:
  7.2 148.5 %copy-start = (bf16[2560,64]{0,1:T(8,128)(2,1)S(1)}, bf16[2560,64]{0,1:T(8,128)(2,1)}, u32[]{:S(2)}) copy-start(bf16[2560,64]{0,1:T(8,128)(2,1)} %param.26) | copy-start | bytes 983044
  7.2 117.2 %all-gather.3.cloned.1.call-start = ((), (), s32[]{:S(2)}) async-start(), calls=%async_computation.5 | async-start | bytes 1474560 | tf_op jit(solution)/shard_map/all_gather | solution.py:109
  38.8 1.5 copy-start.3
  41.2 19.0 %copy-start.6 = (bf16[1,128,256]{2,1,0:T(8,128)(2,1)S(1)}, bf16[1,128,256]{2,1,0:T(8,128)(2,1)}, u32[]{:S(2)}) copy-start(bf16[1,128,256]{2,1,0:T(8,128)(2,1)} %param.20) | copy-start | bytes 196612
  55.5 14.9 %copy-start.7 = (bf16[1,128,256]{2,1,0:T(8,128)(2,1)S(1)}, bf16[1,128,256]{2,1,0:T(8,128)(2,1)}, u32[]{:S(2)}) copy-start(bf16[1,128,256]{2,1,0:T(8,128)(2,1)} %param.21) | copy-start | bytes 196612
  56.8 23.9 %all-to-all-start.3 = ((bf16[4,2,10240]{2,1,0:T(2,128)(2,1)}), bf16[4,2,10240]{2,1,0:T(2,128)(2,1)S(1)}, u32[]{:S(2)}, u32[]{:S(2)}) async-start(bf16[4,2,10240]{2,1,0:T(2,128)(2,1)} %reshape.115), calls=%async_computation.3 | async-start | bytes 327680 | tf_op jit(solution)/shard_map/all_to_all | solution.py:103
  60.2 70.2 %all-gather.5.cloned.1.call-start = ((), (), s32[]{:S(2)}) async-start(), calls=%async_computation.6 | async-start | bytes 1474560 | tf_op jit(solution)/shard_map/all_gather | solution.py:110
  70.3 10.1 %copy-start.8 = (bf16[1,128,256]{2,1,0:T(8,128)(2,1)S(1)}, bf16[1,128,256]{2,1,0:T(8,128)(2,1)}, u32[]{:S(2)}) copy-start(bf16[1,128,256]{2,1,0:T(8,128)(2,1)} %param.19) | copy-start | bytes 196612
  83.0 10.0 %copy-start.4 = (bf16[1,32,2560]{2,1,0:T(8,128)(2,1)S(1)}, bf16[1,32,2560]{2,1,0:T(8,128)(2,1)}, u32[]{:S(2)}) copy-start(bf16[1,32,2560]{2,1,0:T(8,128)(2,1)} %param.16) | copy-start | bytes 491524
  87.3 23.7 %all-to-all-start = ((bf16[4,2,4096]{2,1,0:T(2,128)(2,1)}), bf16[4,2,4096]{2,1,0:T(2,128)(2,1)S(1)}, u32[]{:S(2)}, u32[]{:S(2)}) async-start(bf16[4,2,4096]{2,1,0:T(2,128)(2,1)} %reshape.109), calls=%async_computation | async-start | bytes 131072 | tf_op jit(solution)/shard_map/all_to_all | solution.py:122
  111.0 11.5 %all-to-all-start.2 = ((bf16[4,2,10240]{2,1,0:T(2,128)(2,1)}), bf16[4,2,10240]{2,1,0:T(2,128)(2,1)S(1)}, u32[]{:S(2)}, u32[]{:S(2)}) async-start(bf16[4,2,10240]{2,1,0:T(2,128)(2,1)} %reshape.113), calls=%async_computation.2 | async-start | bytes 327680 | tf_op jit(solution)/shard_map/all_to_all | solution.py:101
  116.5 0.7 copy-start.1
  142.8 6.0 %copy-start.2 = (f32[1,128,256]{2,1,0:T(8,128)S(1)}, f32[1,128,256]{2,1,0:T(8,128)}, u32[]{:S(2)}) copy-start(f32[1,128,256]{2,1,0:T(8,128)} %copy-done.1) | copy-start | bytes 393220
  142.8 6.1 %copy-start.5 = (bf16[1024,64]{0,1:T(8,128)(2,1)S(1)}, bf16[1024,64]{0,1:T(8,128)(2,1)}, u32[]{:S(2)}) copy-start(bf16[1024,64]{0,1:T(8,128)(2,1)} %param.27) | copy-start | bytes 393220
  145.4 9.3 %all-to-all-start.4 = ((bf16[4,2,10240]{2,1,0:T(2,128)(2,1)}), bf16[4,2,10240]{2,1,0:T(2,128)(2,1)S(1)}, u32[]{:S(2)}, u32[]{:S(2)}) async-start(bf16[4,2,10240]{2,1,0:T(2,128)(2,1)} %reshape.117), calls=%async_computation.4 | async-start | bytes 327680 | tf_op jit(solution)/shard_map/all_to_all | solution.py:121
  154.9 0.8 copy-start.9
Sparse Core Ops, SparseCore 0:
  40.4 23.5 all-gather.2
  83.1 25.0 all-gather.4
where the time goes:
time: 165 us; the launch traced here: 164 us
  other arithmetic  48.4 us (29%)
  local copies, waits for them, and re-layouts  33 us (20%)
  blocking collectives  33 us (20%)
  starting transfers between devices  16.9 us (10%)
  between operations  15.3 us (9%)
  waiting for transfers between devices  10.9 us (7%)
  matrix products  5.96 us (4%)
    unnamed x11, other arithmetic  45.5 us
    unnamed x41, local copies, waits for them, and re-layouts  18.6 us
    all_to_all x1, blocking collectives, on_device(): lax.all_to_all(main_key, 'grp', split_axis=2, concat_axis=1, tiled=True)  13.1 us
    all_gather x1, blocking collectives, on_device(): lax.all_gather(guide_key, 'seq', axis=1, tiled=True)  10 us
    all_gather x1, blocking collectives, on_device(): lax.all_gather(guide_value, 'seq', axis=1, tiled=True)  9.84 us
    all_to_all x1, waiting for transfers between devices, on_device(): lax.all_to_all(main_out[None], 'grp', split_axis=1, concat_axis=2, tiled=...  5.51 us
    all_to_all x1, waiting for transfers between devices, on_device(): lax.all_to_all(main_query, 'grp', split_axis=2, concat_axis=1, tiled=True)  5.28 us
    all_to_all x1, starting transfers between devices, on_device(): lax.all_to_all(main_query, 'grp', split_axis=2, concat_axis=1, tiled=True)  5.1 us
  transfers between devices with their start and end apart: 6, of which 2 were waited for; matrix products, arithmetic and copies ran while one was open for 31% of the time, Pallas kernels for 0%

commit v1 on v0

v1 whole, which is shorter than its diff:
```python
import functools
import math

import jax
import jax.numpy as jnp
from jax import lax
from jax.experimental import pallas as pl
from jax.experimental.pallas import tpu as pltpu
from jax.sharding import PartitionSpec as P

HD = 128
HM = 20
STEPS = 50
SLOTS = 8

guidance = 2.5
flow_shift = 3.0
epsilon = 1e-06

KEY, QUERY, VALUE = 0, 1, 2


def sigma_at(index):
    remaining = 1.0 - index.astype(jnp.float32) / STEPS
    return flow_shift * remaining / (1.0 + (flow_shift - 1.0) * remaining)


def aligned(value, multiple):
    return pl.multiple_of(value, multiple)


def wait_for(ref, sem):
    pltpu.make_async_copy(ref, ref, sem).wait()


def loop(count, body):
    if count <= 8:
        for i in range(count):
            body(i)
    else:
        pl.loop(0, count)(body)


def project(pieces, row, weight_ref):
    width = sum(piece.shape[1] for piece in pieces)
    center = sum(jnp.sum(piece, axis=-1, keepdims=True) for piece in pieces) * (1.0 / width)
    centered = [piece - center for piece in pieces]
    spread = sum(jnp.sum(piece * piece, axis=-1, keepdims=True) for piece in centered) * (1.0 / width)
    scale = lax.rsqrt(spread + epsilon)
    total = None
    start = 0
    for piece in centered:
        part = slice(start, start + piece.shape[1])
        start += piece.shape[1]
        wide = piece * scale * (1.0 + row[1:2, part]) + row[0:1, part]
        high = wide.astype(jnp.bfloat16)
        rest = wide - high.astype(jnp.float32)
        middle = rest.astype(jnp.bfloat16)
        low = (rest - middle.astype(jnp.float32)).astype(jnp.bfloat16)
        product = jnp.dot(
            jnp.concatenate([high, middle, low], axis=0),
            weight_ref[part, :],
            preferred_element_type=jnp.float32,
        )
        total = product if total is None else total + product
    rows = total.shape[0] // 3
    return total[:rows] + total[rows : 2 * rows] + total[2 * rows :]


def kernel(
    G, S, R, main_heads, guide_heads,
    step_ref, main_q, main_k, main_v, guide_q, guide_k, guide_v,
    main_mod, guide_mod, main_head, guide_head,
    main_flow, guide_flow,
    moved, keys, queries, values, weights, sums, attended, returned, final,
    main_table, guide_table, main_weight, guide_weight,
    table_sem, z_recv, z_send, p_recv, p_send, o_recv, o_send, f_recv, f_send,
):
    g = lax.axis_index("grp")
    s = lax.axis_index("seq")
    rows = main_q.shape[1]
    block = guide_q.shape[1]
    tokens = keys.shape[0]
    count = queries.shape[0]
    blocks = count // block
    heads = main_heads + guide_heads
    wide = main_heads * HD
    slot = s // R
    part = s % R

    tables = (
        (main_mod, main_table), (guide_mod, guide_table),
        (main_head, main_weight), (guide_head, guide_weight),
    )

    barrier = pltpu.get_barrier_semaphore()
    for d in range(1, G):
        pl.semaphore_signal(barrier, inc=1, device_id={"grp": (g + d) % G})

    def greet(i):
        pl.semaphore_signal(barrier, inc=1, device_id={"seq": (s + 1 + i) % S})

    loop(S - 1, greet)

    sources = (main_k, main_q, main_v)
    my_rows = pl.ds(aligned(g * rows, rows), rows)
    for a in range(3):
        pltpu.make_async_copy(
            sources[a].at[0, :, pl.ds(aligned(g * wide, HD), wide)],
            moved.at[a, my_rows, :],
            z_recv.at[a],
        ).start()

    pl.semaphore_wait(barrier, G - 1 + S - 1)

    def send_z(a):
        for d in range(1, G):
            peer = (g + d) % G
            pltpu.make_async_remote_copy(
                src_ref=sources[a].at[0, :, pl.ds(aligned(peer * wide, HD), wide)],
                dst_ref=moved.at[a, my_rows, :],
                send_sem=z_send,
                recv_sem=z_recv.at[a],
                device_id={"grp": peer},
            ).start()

    targets = (keys, queries, values)

    def plane(a, source, first, number, act):
        def one(index):
            head = (index + s) % number
            src = source.at[:, pl.ds(aligned(head * HD, HD), HD)]
            if a == QUERY:
                dst = targets[a].at[pl.ds(aligned((s % blocks) * block, block), block), :]
            else:
                dst = targets[a].at[pl.ds(aligned(s * block, block), block), :]

            def to(unit):
                act(a, src, dst, unit)

            if a == QUERY:
                to((first + head) * R + s // blocks)
            else:
                loop(R, lambda r: to((first + head) * R + r))

        loop(number, one)

    def start(a, src, dst, unit):
        @pl.when(unit == s)
        def _():
            pltpu.make_async_copy(src, dst, p_recv.at[a]).start()

        @pl.when(unit != s)
        def _():
            pltpu.make_async_remote_copy(
                src_ref=src, dst_ref=dst, send_sem=p_send, recv_sem=p_recv.at[a],
                device_id={"seq": unit},
            ).start()

    def sent(a, src, dst, unit):
        @pl.when(unit != s)
        def _():
            wait_for(dst, p_send)

    guide_sources = (guide_k.at[0], guide_q.at[0], guide_v.at[0])
    send_z(KEY)
    plane(KEY, guide_sources[KEY], main_heads, guide_heads, start)
    send_z(QUERY)
    plane(QUERY, guide_sources[QUERY], main_heads, guide_heads, start)
    send_z(VALUE)
    plane(VALUE, guide_sources[VALUE], main_heads, guide_heads, start)
    for i, (src, dst) in enumerate(tables):
        pltpu.make_async_copy(src, dst, table_sem.at[i]).start()
    for a in range(3):
        wait_for(moved.at[a], z_recv.at[a])
        plane(a, moved.at[a], 0, main_heads, start)

    factor = math.log2(math.e) / math.sqrt(HD)
    score_rows = max(32, min(256, 256 * 1024 // tokens))
    value_rows = min(256, count)

    @pl.when(slot < heads)
    def _():
        wait_for(keys, p_recv.at[KEY])
        wait_for(queries, p_recv.at[QUERY])

        def score(i):
            at = pl.ds(i * score_rows, score_rows)
            scores = lax.dot_general(
                queries[at, :], keys[...], (((1,), (1,)), ((), ())),
                preferred_element_type=jnp.float32,
            )
            highest = jnp.max(scores, axis=-1, keepdims=True)
            unrounded = jnp.exp2((scores - highest) * factor)
            sums[at, :] = jnp.broadcast_to(
                jnp.sum(unrounded, axis=-1, keepdims=True), (score_rows, HD)
            )
            weights[at, :] = unrounded.astype(jnp.bfloat16)

        loop(count // score_rows, score)
        wait_for(values, p_recv.at[VALUE])
        columns = pl.ds(aligned(slot * HD, HD), HD)
        for i in range(count // value_rows):
            at = pl.ds(i * value_rows, value_rows)
            summed = jnp.dot(weights[at, :], values[...], preferred_element_type=jnp.float32)
            attended[at, :] = (summed / sums[at, :]).astype(jnp.bfloat16)
            for b in range(i * value_rows // block, (i + 1) * value_rows // block):
                src = attended.at[pl.ds(b * block, block), :]
                dst = returned.at[:, columns]
                owner = part * blocks + b

                @pl.when(owner == s)
                def _():
                    pltpu.make_async_copy(src, dst, o_recv).start()

                @pl.when(owner != s)
                def _():
                    pltpu.make_async_remote_copy(
                        src_ref=src, dst_ref=dst, send_sem=o_send, recv_sem=o_recv,
                        device_id={"seq": owner},
                    ).start()

    wait_for(returned, o_recv)
    pltpu.make_async_copy(returned.at[my_rows, :], final.at[g], f_recv).start()
    for d in range(1, G):
        peer = (g + d) % G
        pltpu.make_async_remote_copy(
            src_ref=returned.at[pl.ds(aligned(peer * rows, rows), rows), :],
            dst_ref=final.at[g],
            send_sem=f_send,
            recv_sem=f_recv,
            device_id={"grp": peer},
        ).start()

    for a in range(3):
        wait_for(moved.at[a, pl.ds(0, (G - 1) * rows), :], z_send)
        plane(a, guide_sources[a], main_heads, guide_heads, sent)
        plane(a, moved.at[a], 0, main_heads, sent)

    @pl.when(slot < heads)
    def _():
        for b in range(blocks):
            @pl.when(part * blocks + b != s)
            def _():
                wait_for(attended.at[pl.ds(b * block, block), :], o_send)

    for i, (src, dst) in enumerate(tables):
        pltpu.make_async_copy(src, dst, table_sem.at[i]).wait()
    step_now = step_ref[0]
    main_row = main_table[step_now].astype(jnp.float32)
    guide_row = guide_table[step_now].astype(jnp.float32)
    wait_for(final, f_recv)
    main_flow[...] = project(
        [final[i, :, :wide].astype(jnp.float32) for i in range(G)], main_row, main_weight
    )
    guide_flow[...] = project(
        [final[i, :, wide:].astype(jnp.float32) for i in range(G)], guide_row, guide_weight
    )
    wait_for(final.at[pl.ds(0, G - 1)], f_send)


def on_device(G, S, *arguments):
    (main_query, main_key, main_value, guide_query, guide_key, guide_value,
     latents, step_index, main_mod, guide_mod, main_head, guide_head) = arguments
    R = max(1, S // SLOTS)
    main_heads = HM // G
    guide_heads = guide_query.shape[2] // HD
    heads = main_heads + guide_heads
    rows = main_query.shape[1]
    block = guide_query.shape[1]
    tokens = S * block
    count = tokens // R
    channels = main_head.shape[1]
    bf16 = jnp.bfloat16
    anywhere = pl.BlockSpec(memory_space=pl.ANY)
    vmem = pl.BlockSpec(memory_space=pltpu.VMEM)
    dma = pltpu.SemaphoreType.DMA
    main_flow, guide_flow = pl.pallas_call(
        functools.partial(kernel, G, S, R, main_heads, guide_heads),
        out_shape=[jax.ShapeDtypeStruct((rows, channels), jnp.float32)] * 2,
        in_specs=[pl.BlockSpec(memory_space=pltpu.SMEM)] + [anywhere] * 10,
        out_specs=[vmem, vmem],
        scratch_shapes=[
            pltpu.VMEM((3, block, main_heads * HD), bf16),
            pltpu.VMEM((tokens, HD), bf16),
            pltpu.VMEM((count, HD), bf16),
            pltpu.VMEM((tokens, HD), bf16),
            pltpu.VMEM((count, tokens), bf16),
            pltpu.VMEM((count, HD), jnp.float32),
            pltpu.VMEM((count, HD), bf16),
            pltpu.VMEM((block, heads * HD), bf16),
            pltpu.VMEM((G, rows, heads * HD), bf16),
            pltpu.VMEM(main_mod.shape, bf16),
            pltpu.VMEM(guide_mod.shape, bf16),
            pltpu.VMEM(main_head.shape, bf16),
            pltpu.VMEM(guide_head.shape, bf16),
            dma((4,)), dma((3,)), dma, dma((3,)), dma, dma, dma, dma, dma,
        ],
        compiler_params=pltpu.CompilerParams(
            collective_id=0, has_side_effects=True, vmem_limit_bytes=48 * 1024 * 1024
        ),
        cost_estimate=pl.CostEstimate(
            flops=4 * count * tokens * HD, bytes_accessed=4 * tokens * HD * 2,
            transcendentals=count * tokens,
        ),
    )(
        step_index, main_query, main_key, main_value, guide_query, guide_key, guide_value,
        main_mod, guide_mod, main_head, guide_head,
    )
    step_now = step_index[0]
    velocity = (guide_flow + guidance * (main_flow - guide_flow))[None]
    advanced = latents + (sigma_at(step_now + 1) - sigma_at(step_now)) * velocity
    return (velocity, advanced)


def solution(mesh):
    return jax.shard_map(
        functools.partial(on_device, mesh.shape["grp"], mesh.shape["seq"]),
        mesh=mesh,
        in_specs=(
            P("seq", "grp", None),
            P("seq", "grp", None),
            P("seq", "grp", None),
            P("seq", None, "grp"),
            P("seq", None, "grp"),
            P("seq", None, "grp"),
            P("seq", "grp", None),
            P(),
            P(),
            P(),
            P(),
            P(),
        ),
        out_specs=(P("seq", "grp", None), P("seq", "grp", None)),
        check_vma=False,
    )
```

time: 165 us -> 41.3 us (0.25)
  the two profiles are of different devices: /device:TPU:0 before, /device:TPU:29 now
where the time goes in v1:
time: 41.3 us; the launch traced here: 41.1 us
  Pallas kernels  34.3 us (83%)
  local copies, waits for them, and re-layouts  3.98 us (10%)
  between operations  1.51 us (4%)
  other arithmetic  1.23 us (3%)
    pallas_call x1, Pallas kernels, on_device(): pl.pallas_call(functools.partial(kernel, G, S, R, main_heads, guide_heads...  34.3 us
    unnamed x20, local copies, waits for them, and re-layouts  3.98 us

profile of v1, /device:TPU:29, one launch (start us, length us, event | category | flops | bytes accessed | tf_op | source)
XLA Modules:
  0.0 41.1 jit_solution(11981168341945103714)
XLA Ops:
  1.3 0.0 copy-start
  1.3 0.0 copy-start.3
  1.3 0.0 copy-start.4
  1.3 0.0 copy-start.5
  1.3 0.0 copy-start.6
  1.3 1.4 %copy.14.main_head = bf16[2560,64]{1,0:T(8,128)(2,1)S(1)} copy(bf16[2560,64]{0,1:T(8,128)(2,1)} %param.22) | data formatting | bytes 655360 | tf_op args[10]
  2.7 0.0 copy-start.1
  2.7 0.0 copy-start.2
  2.7 1.1 %copy.15.guide_head = bf16[1024,64]{1,0:T(8,128)(2,1)S(1)} copy(bf16[1024,64]{0,1:T(8,128)(2,1)} %param.23) | data formatting | bytes 262144 | tf_op args[11]
  3.9 0.0 copy-done
  3.9 0.0 copy-done.3
  3.9 0.0 copy-done.4
  3.9 0.0 copy-done.5
  3.9 0.0 copy-done.6
  3.9 0.0 copy-done.1
  3.9 0.0 copy-done.2
  3.9 0.0 copy-start.7
  3.9 0.8 %copy-done.7 = bf16[1,128,256]{2,1,0:T(8,128)(2,1)S(1)} copy-done((bf16[1,128,256]{2,1,0:T(8,128)(2,1)S(1)}, bf16[1,128,256]{2,1,0:T(8,128)(2,1)}, u32[]{:S(2)}) %copy-start.7) | copy-done | bytes 65560
  4.8 34.3 %shard_map.131 = (f32[32,64]{1,0:T(8,128)S(1)}, f32[32,64]{1,0:T(8,128)S(1)}) custom-call(s32[1]{0:T(128)S(6)} %copy.16.step_ref, bf16[1,32,2560]{2,1,0:T(8,128)(2,1)S(1)} %copy-done.2, bf16[1,32,2560]{2,1,0:T(8,128)(2,1)S(1)} %copy-done.3, bf16[1,32,2560]{2,1,0:T(8,128)(2,1)S(1)} %copy-done.4, bf16[1,128,256]{2,1,0:T(8,128)(2,1)S(1)} %copy-done.5, ...), custom_call_target="tpu_custom_call" | custom-call | flops 536870912 | bytes 1048576 | tf_op jit(solution)/shard_map/pallas_call | solution.py:278
  39.1 0.6 %fusion = f32[1,32,64]{2,1,0:T(8,128)} fusion(f32[32,64]{1,0:T(8,128)S(1)} %get-tuple-element.4, f32[32,64]{1,0:T(8,128)S(1)} %get-tuple-element.5), kind=kLoop, calls=%fused_computation.2 | loop fusion | flops 6144 | bytes 24576 | tf_op jit(solution)/shard_map/broadcast_in_dim | solution.py:311
  39.7 0.0 copy-start.8
  39.8 0.6 %copy-done.8 = f32[1,32,64]{2,1,0:T(8,128)S(1)} copy-done((f32[1,32,64]{2,1,0:T(8,128)S(1)}, f32[1,32,64]{2,1,0:T(8,128)}, u32[]{:S(2)}) %copy-start.8) | copy-done | bytes 8216
  40.4 0.6 %bitcast_add_fusion = f32[1,32,64]{2,1,0:T(8,128)} fusion(f32[1,32,64]{2,1,0:T(8,128)S(1)} %copy-done.8, f32[]{:T(128)} %bitcast.1, f32[32,64]{1,0:T(8,128)S(1)} %get-tuple-element.4, f32[32,64]{1,0:T(8,128)S(1)} %get-tuple-element.5), kind=kLoop, calls=%fused_computation | loop fusion | flops 10240 | bytes 32772 | tf_op jit(solution)/shard_map/add | solution.py:312
Async XLA Ops:
  1.3 2.6 %copy-start = (bf16[50,2,2560]{2,1,0:T(2,128)(2,1)S(1)}, bf16[50,2,2560]{2,1,0:T(2,128)(2,1)}, u32[]{:S(2)}) copy-start(bf16[50,2,2560]{2,1,0:T(2,128)(2,1)} %main_mod.1) | copy-start | bytes 1536004
  1.3 2.6 %copy-start.3 = (bf16[1,32,2560]{2,1,0:T(8,128)(2,1)S(1)}, bf16[1,32,2560]{2,1,0:T(8,128)(2,1)}, u32[]{:S(2)}) copy-start(bf16[1,32,2560]{2,1,0:T(8,128)(2,1)} %main_k.1) | copy-start | bytes 491524
  1.3 2.6 %copy-start.4 = (bf16[1,32,2560]{2,1,0:T(8,128)(2,1)S(1)}, bf16[1,32,2560]{2,1,0:T(8,128)(2,1)}, u32[]{:S(2)}) copy-start(bf16[1,32,2560]{2,1,0:T(8,128)(2,1)} %main_v.1) | copy-start | bytes 491524
  1.3 2.6 %copy-start.5 = (bf16[1,128,256]{2,1,0:T(8,128)(2,1)S(1)}, bf16[1,128,256]{2,1,0:T(8,128)(2,1)}, u32[]{:S(2)}) copy-start(bf16[1,128,256]{2,1,0:T(8,128)(2,1)} %guide_q.1) | copy-start | bytes 196612
  1.3 2.6 %copy-start.6 = (bf16[1,128,256]{2,1,0:T(8,128)(2,1)S(1)}, bf16[1,128,256]{2,1,0:T(8,128)(2,1)}, u32[]{:S(2)}) copy-start(bf16[1,128,256]{2,1,0:T(8,128)(2,1)} %guide_k.1) | copy-start | bytes 196612
  2.7 1.2 %copy-start.1 = (bf16[50,2,1024]{2,1,0:T(2,128)(2,1)S(1)}, bf16[50,2,1024]{2,1,0:T(2,128)(2,1)}, u32[]{:S(2)}) copy-start(bf16[50,2,1024]{2,1,0:T(2,128)(2,1)} %guide_mod.1) | copy-start | bytes 614404
  2.7 1.2 %copy-start.2 = (bf16[1,32,2560]{2,1,0:T(8,128)(2,1)S(1)}, bf16[1,32,2560]{2,1,0:T(8,128)(2,1)}, u32[]{:S(2)}) copy-start(bf16[1,32,2560]{2,1,0:T(8,128)(2,1)} %main_q.1) | copy-start | bytes 491524
  3.9 0.8 %copy-start.7 = (bf16[1,128,256]{2,1,0:T(8,128)(2,1)S(1)}, bf16[1,128,256]{2,1,0:T(8,128)(2,1)}, u32[]{:S(2)}) copy-start(bf16[1,128,256]{2,1,0:T(8,128)(2,1)} %guide_v.1) | copy-start | bytes 196612
  39.7 0.7 %copy-start.8 = (f32[1,32,64]{2,1,0:T(8,128)S(1)}, f32[1,32,64]{2,1,0:T(8,128)}, u32[]{:S(2)}) copy-start(f32[1,32,64]{2,1,0:T(8,128)} %param.18) | copy-start | bytes 24580

commit v2 on v1

--- a/solution.py
+++ b/solution.py
@@ -57,9 +57,10 @@
         rest = wide - high.astype(jnp.float32)
         middle = rest.astype(jnp.bfloat16)
         low = (rest - middle.astype(jnp.float32)).astype(jnp.bfloat16)
-        product = jnp.dot(
+        product = lax.dot_general(
             jnp.concatenate([high, middle, low], axis=0),
-            weight_ref[part, :],
+            weight_ref[:, part],
+            (((1,), (1,)), ((), ())),
             preferred_element_type=jnp.float32,
         )
         total = product if total is None else total + product
@@ -70,10 +71,10 @@
 def kernel(
     G, S, R, main_heads, guide_heads,
     step_ref, main_q, main_k, main_v, guide_q, guide_k, guide_v,
-    main_mod, guide_mod, main_head, guide_head,
-    main_flow, guide_flow,
+    main_mod, guide_mod, main_head, guide_head, latents,
+    velocity, advanced,
     moved, keys, queries, values, weights, sums, attended, returned, final,
-    main_table, guide_table, main_weight, guide_weight,
+    main_table, guide_table, main_weight, guide_weight, held_latents,
     table_sem, z_recv, z_send, p_recv, p_send, o_recv, o_send, f_recv, f_send,
 ):
     g = lax.axis_index("grp")
@@ -91,6 +92,7 @@
     tables = (
         (main_mod, main_table), (guide_mod, guide_table),
         (main_head, main_weight), (guide_head, guide_weight),
+        (latents, held_latents),
     )
 
     barrier = pltpu.get_barrier_semaphore()
@@ -250,12 +252,16 @@
     main_row = main_table[step_now].astype(jnp.float32)
     guide_row = guide_table[step_now].astype(jnp.float32)
     wait_for(final, f_recv)
-    main_flow[...] = project(
+    main_flow = project(
         [final[i, :, :wide].astype(jnp.float32) for i in range(G)], main_row, main_weight
     )
-    guide_flow[...] = project(
+    guide_flow = project(
         [final[i, :, wide:].astype(jnp.float32) for i in range(G)], guide_row, guide_weight
     )
+    mixed = guide_flow + guidance * (main_flow - guide_flow)
+    index = jnp.full((1, mixed.shape[1]), step_now, jnp.int32)
+    velocity[0] = mixed
+    advanced[0] = held_latents[0] + (sigma_at(index + 1) - sigma_at(index)) * mixed
     wait_for(final.at[pl.ds(0, G - 1)], f_send)
 
 
@@ -270,15 +276,14 @@
     block = guide_query.shape[1]
     tokens = S * block
     count = tokens // R
-    channels = main_head.shape[1]
     bf16 = jnp.bfloat16
-    anywhere = pl.BlockSpec(memory_space=pl.ANY)
+    anywhere = pl.BlockSpec(memory_space=pltpu.HBM)
     vmem = pl.BlockSpec(memory_space=pltpu.VMEM)
     dma = pltpu.SemaphoreType.DMA
-    main_flow, guide_flow = pl.pallas_call(
+    return pl.pallas_call(
         functools.partial(kernel, G, S, R, main_heads, guide_heads),
-        out_shape=[jax.ShapeDtypeStruct((rows, channels), jnp.float32)] * 2,
-        in_specs=[pl.BlockSpec(memory_space=pltpu.SMEM)] + [anywhere] * 10,
+        out_shape=[jax.ShapeDtypeStruct(latents.shape, jnp.float32)] * 2,
+        in_specs=[pl.BlockSpec(memory_space=pltpu.SMEM)] + [anywhere] * 11,
         out_specs=[vmem, vmem],
         scratch_shapes=[
             pltpu.VMEM((3, block, main_heads * HD), bf16),
@@ -292,12 +297,13 @@
             pltpu.VMEM((G, rows, heads * HD), bf16),
             pltpu.VMEM(main_mod.shape, bf16),
             pltpu.VMEM(guide_mod.shape, bf16),
-            pltpu.VMEM(main_head.shape, bf16),
-            pltpu.VMEM(guide_head.shape, bf16),
-            dma((4,)), dma((3,)), dma, dma((3,)), dma, dma, dma, dma, dma,
+            pltpu.VMEM(main_head.shape[::-1], bf16),
+            pltpu.VMEM(guide_head.shape[::-1], bf16),
+            pltpu.VMEM(latents.shape, jnp.float32),
+            dma((5,)), dma((3,)), dma, dma((3,)), dma, dma, dma, dma, dma,
         ],
         compiler_params=pltpu.CompilerParams(
-            collective_id=0, has_side_effects=True, vmem_limit_bytes=48 * 1024 * 1024
+            collective_id=0, has_side_effects=True, vmem_limit_bytes=60 * 1024 * 1024
         ),
         cost_estimate=pl.CostEstimate(
             flops=4 * count * tokens * HD, bytes_accessed=4 * tokens * HD * 2,
@@ -305,12 +311,8 @@
         ),
     )(
         step_index, main_query, main_key, main_value, guide_query, guide_key, guide_value,
-        main_mod, guide_mod, main_head, guide_head,
-    )
-    step_now = step_index[0]
-    velocity = (guide_flow + guidance * (main_flow - guide_flow))[None]
-    advanced = latents + (sigma_at(step_now + 1) - sigma_at(step_now)) * velocity
-    return (velocity, advanced)
+        main_mod, guide_mod, main_head.T, guide_head.T, latents,
+    )
 
 
 def solution(mesh):

time: 41.3 us -> 38.5 us (0.932)
  local copies, waits for them, and re-layouts: 3.98 us -> 1.94 us
  other arithmetic: 1.23 us -> 0 us
  Pallas kernels: 34.3 us -> 35.1 us
    unnamed x20 -> x4, local copies, waits for them, and re-layouts: 3.98 us -> 1.94 us
    pallas_call x1, Pallas kernels: 34.3 us -> 35.1 us  [on_device(): pl.pallas_call(functools.partial(kernel, G, S, R, main_heads, guide_heads...]
    add x1 -> x0, other arithmetic: 0.61 us -> none  [on_device(): latents + (sigma_at(step_now + 1) - sigma_at(step_now)) * velocity]
    broadcast_in_dim x1 -> x0, other arithmetic: 0.61 us -> none  [on_device(): velocity = (guide_flow + guidance * (main_flow - guide_flow))[None]]
where the time goes in v2:
time: 38.5 us; the launch traced here: 38.3 us
  Pallas kernels  35.1 us (91%)
  local copies, waits for them, and re-layouts  1.94 us (5%)
  between operations  1.3 us (3%)
    pallas_call x1, Pallas kernels, on_device(): pl.pallas_call(functools.partial(kernel, G, S, R, main_heads, guide_heads...  35.1 us
    unnamed x4, local copies, waits for them, and re-layouts  1.94 us

profile of v2, /device:TPU:29, one launch (start us, length us, event | category | flops | bytes accessed | tf_op | source)
XLA Modules:
  0.0 38.3 jit_solution(14243242875764094923)
XLA Ops:
  1.3 35.1 %shard_map.131 = (f32[1,32,64]{2,1,0:T(8,128)}, f32[1,32,64]{2,1,0:T(8,128)}) custom-call(s32[1]{0:T(128)S(6)} %copy.16.step_ref, bf16[1,32,2560]{2,1,0:T(8,128)(2,1)} %main_q.1, bf16[1,32,2560]{2,1,0:T(8,128)(2,1)} %main_k.1, bf16[1,32,2560]{2,1,0:T(8,128)(2,1)} %main_v.1, bf16[1,128,256]{2,1,0:T(8,128)(2,1)} %guide_q.1, bf16[1,128,256]{2,1,0:T(8,128)(2,1)} %guide_k.1, ...), custom_call_target="tpu_custom_call" | custom-call | flops 536870912 | bytes 1048576 | tf_op jit(solution)/shard_map/pallas_call | solution.py:283
  36.4 0.0 copy-start
  36.4 1.3 %copy.17 = f32[1,32,64]{2,1,0:T(8,128)} copy(f32[1,32,64]{2,1,0:T(8,128)} %get-tuple-element.4) | data formatting | bytes 16384
  37.7 0.0 copy-done
  37.7 0.6 %copy.18 = f32[1,32,64]{2,1,0:T(8,128)} copy(f32[1,32,64]{2,1,0:T(8,128)S(1)} %copy-done) | data formatting | bytes 16384
Async XLA Ops:
  36.4 1.3 %copy-start = (f32[1,32,64]{2,1,0:T(8,128)S(1)}, f32[1,32,64]{2,1,0:T(8,128)}, u32[]{:S(2)}) copy-start(f32[1,32,64]{2,1,0:T(8,128)} %get-tuple-element.5) | copy-start | bytes 24580

commit v3 on v2

v3 whole, which is shorter than its diff:
```python
import functools
import math

import jax
import jax.numpy as jnp
from jax import lax
from jax.experimental import pallas as pl
from jax.experimental.pallas import tpu as pltpu
from jax.sharding import PartitionSpec as P

HD = 128
HM = 20
STEPS = 50
SLOTS = 8

guidance = 2.5
flow_shift = 3.0
epsilon = 1e-06

KEY, QUERY, VALUE = 0, 1, 2


def sigma_at(index):
    remaining = 1.0 - index.astype(jnp.float32) / STEPS
    return flow_shift * remaining / (1.0 + (flow_shift - 1.0) * remaining)


def aligned(value, multiple):
    return pl.multiple_of(value, multiple)


def wait_for(ref, sem):
    pltpu.make_async_copy(ref, ref, sem).wait()


def loop(count, body):
    if count <= 8:
        for i in range(count):
            body(i)
    else:
        pl.loop(0, count)(body)


def project(pieces, row, weight_ref):
    width = sum(piece.shape[1] for piece in pieces)
    center = sum(jnp.sum(piece, axis=-1, keepdims=True) for piece in pieces) * (1.0 / width)
    centered = [piece - center for piece in pieces]
    spread = sum(jnp.sum(piece * piece, axis=-1, keepdims=True) for piece in centered) * (1.0 / width)
    scale = lax.rsqrt(spread + epsilon)
    total = None
    start = 0
    for piece in centered:
        part = slice(start, start + piece.shape[1])
        start += piece.shape[1]
        wide = piece * scale * (1.0 + row[1:2, part]) + row[0:1, part]
        high = wide.astype(jnp.bfloat16)
        rest = wide - high.astype(jnp.float32)
        middle = rest.astype(jnp.bfloat16)
        low = (rest - middle.astype(jnp.float32)).astype(jnp.bfloat16)
        product = lax.dot_general(
            jnp.concatenate([high, middle, low], axis=0),
            weight_ref[:, part],
            (((1,), (1,)), ((), ())),
            preferred_element_type=jnp.float32,
        )
        total = product if total is None else total + product
    rows = total.shape[0] // 3
    return total[:rows] + total[rows : 2 * rows] + total[2 * rows :]


def kernel(
    G, S, R, main_heads, guide_heads,
    step_ref, main_q, main_k, main_v, guide_q, guide_k, guide_v,
    main_mod, guide_mod, main_head, guide_head, latents,
    velocity, advanced,
    keys, queries, values, weights, sums, attended, final,
    main_table, guide_table, main_weight, guide_weight, held_latents,
    table_sem, recv, send, o_recv, o_send,
):
    g = lax.axis_index("grp")
    s = lax.axis_index("seq")
    rows = main_q.shape[1]
    block = guide_q.shape[1]
    tokens = keys.shape[0]
    count = queries.shape[0]
    blocks = count // block
    heads = main_heads + guide_heads
    half = SLOTS // 2
    unit = (s + 2 * R * g * (S - 1)) % S
    slot = unit // R
    part = unit % R
    head_here = slot // 2 + half * (slot % 2)

    def owner(plane, head, r):
        place = (2 * head) % SLOTS + head // half
        return (place * R + r + 2 * R * plane) % S

    tables = (
        (main_mod, main_table), (guide_mod, guide_table),
        (main_head, main_weight), (guide_head, guide_weight),
        (latents, held_latents),
    )

    barrier = pltpu.get_barrier_semaphore()

    def greet(i):
        pl.semaphore_signal(
            barrier, inc=1,
            device_id={"grp": (g + (i + 1) // S) % G, "seq": (s + (i + 1) % S) % S},
        )

    loop(G * S - 1, greet)
    pl.semaphore_wait(barrier, G * S - 1)

    main_sources = (main_k.at[0], main_q.at[0], main_v.at[0])
    guide_sources = (guide_k.at[0], guide_q.at[0], guide_v.at[0])
    targets = (keys, queries, values)

    def spread(a, src, dst, plane, head, act):
        if a == QUERY:
            act(a, src, dst, plane, owner(plane, head, s // blocks))
        else:
            loop(R, lambda r: act(a, src, dst, plane, owner(plane, head, r)))

    def place(a):
        return (s % blocks) * block if a == QUERY else s * block

    def main_pieces(a, act):
        number = G * main_heads

        @pl.loop(0, number)
        def _(i):
            column = (i + (g + 1) * main_heads + s) % number
            src = main_sources[a].at[:, pl.ds(aligned(column * HD, HD), HD)]
            dst = targets[a].at[pl.ds(aligned(place(a) + g * rows, rows), rows), :]
            spread(a, src, dst, column // main_heads, column % main_heads, act)

    def guide_pieces(a, act):
        for i in range(guide_heads):
            head = (i + s) % guide_heads
            src = guide_sources[a].at[:, pl.ds(aligned(head * HD, HD), HD)]
            dst = targets[a].at[pl.ds(aligned(place(a), block), block), :]
            spread(a, src, dst, g, main_heads + head, act)

    def start(a, src, dst, plane, seq):
        here = (plane == g) & (seq == s)

        @pl.when(here)
        def _():
            pltpu.make_async_copy(src, dst, recv.at[a]).start()

        @pl.when(jnp.logical_not(here))
        def _():
            pltpu.make_async_remote_copy(
                src_ref=src, dst_ref=dst, send_sem=send, recv_sem=recv.at[a],
                device_id={"grp": plane, "seq": seq},
            ).start()

    def sent(a, src, dst, plane, seq):
        @pl.when(jnp.logical_not((plane == g) & (seq == s)))
        def _():
            wait_for(dst, send)

    for a in range(3):
        main_pieces(a, start)
        guide_pieces(a, start)
    for i, (src, dst) in enumerate(tables):
        pltpu.make_async_copy(src, dst, table_sem.at[i]).start()

    factor = math.log2(math.e) / math.sqrt(HD)
    score_rows = max(32, min(256, 256 * 1024 // tokens))
    value_rows = min(256, count)
    value_blocks = count // value_rows

    @pl.when(head_here < heads)
    def _():
        wait_for(keys, recv.at[KEY])
        wait_for(queries, recv.at[QUERY])

        def score(i):
            at = pl.ds(i * score_rows, score_rows)
            scores = lax.dot_general(
                queries[at, :], keys[...], (((1,), (1,)), ((), ())),
                preferred_element_type=jnp.float32,
            )
            highest = jnp.max(scores, axis=-1, keepdims=True)
            unrounded = jnp.exp2((scores - highest) * factor)
            sums[at, :] = jnp.broadcast_to(
                jnp.sum(unrounded, axis=-1, keepdims=True), (score_rows, HD)
            )
            weights[at, :] = unrounded.astype(jnp.bfloat16)

        loop(count // score_rows, score)
        wait_for(values, recv.at[VALUE])
        column = aligned((g * heads + head_here) * HD, HD)
        for i in range(value_blocks):
            turn = (i + s // 2) % value_blocks
            at = pl.ds(aligned(turn * value_rows, value_rows), value_rows)
            summed = jnp.dot(weights[at, :], values[...], preferred_element_type=jnp.float32)
            attended[at, :] = (summed / sums[at, :]).astype(jnp.bfloat16)
            for b in range(value_rows // block):
                seq = part * blocks + turn * (value_rows // block) + b
                for d in range(G):
                    plane = (g + d + 1) % G
                    first = turn * value_rows + b * block + plane * rows
                    src = attended.at[pl.ds(aligned(first, rows), rows), :]
                    dst = final.at[:, pl.ds(column, HD)]

                    def send_out():
                        pltpu.make_async_remote_copy(
                            src_ref=src, dst_ref=dst, send_sem=o_send, recv_sem=o_recv,
                            device_id={"grp": plane, "seq": seq},
                        ).start()

                    if d < G - 1:
                        send_out()
                    else:
                        @pl.when(seq == s)
                        def _():
                            pltpu.make_async_copy(src, dst, o_recv).start()

                        pl.when(seq != s)(send_out)

    for a in range(3):
        main_pieces(a, sent)
        guide_pieces(a, sent)
    for i, (src, dst) in enumerate(tables):
        pltpu.make_async_copy(src, dst, table_sem.at[i]).wait()
    step_now = step_ref[0]
    main_row = main_table[step_now].astype(jnp.float32)
    guide_row = guide_table[step_now].astype(jnp.float32)
    wait_for(final, o_recv)

    def taken(first, number):
        return [
            final[:, (i * heads + first) * HD : (i * heads + first + number) * HD].astype(jnp.float32)
            for i in range(G)
        ]

    main_flow = project(taken(0, main_heads), main_row, main_weight)
    guide_flow = project(taken(main_heads, guide_heads), guide_row, guide_weight)
    mixed = guide_flow + guidance * (main_flow - guide_flow)
    index = jnp.full((1, mixed.shape[1]), step_now, jnp.int32)
    velocity[0] = mixed
    advanced[0] = held_latents[0] + (sigma_at(index + 1) - sigma_at(index)) * mixed

    @pl.when(head_here < heads)
    def _():
        wait_for(attended.at[pl.ds(0, count - rows), :], o_send)

        @pl.when(s // blocks != part)
        def _():
            wait_for(attended.at[pl.ds(0, rows), :], o_send)


def on_device(G, S, *arguments):
    (main_query, main_key, main_value, guide_query, guide_key, guide_value,
     latents, step_index, main_mod, guide_mod, main_head, guide_head) = arguments
    R = max(1, S // SLOTS)
    main_heads = HM // G
    guide_heads = guide_query.shape[2] // HD
    heads = main_heads + guide_heads
    rows = main_query.shape[1]
    block = guide_query.shape[1]
    tokens = S * block
    count = tokens // R
    bf16 = jnp.bfloat16
    anywhere = pl.BlockSpec(memory_space=pltpu.HBM)
    vmem = pl.BlockSpec(memory_space=pltpu.VMEM)
    dma = pltpu.SemaphoreType.DMA
    return pl.pallas_call(
        functools.partial(kernel, G, S, R, main_heads, guide_heads),
        out_shape=[jax.ShapeDtypeStruct(latents.shape, jnp.float32)] * 2,
        in_specs=[pl.BlockSpec(memory_space=pltpu.SMEM)] + [anywhere] * 11,
        out_specs=[vmem, vmem],
        scratch_shapes=[
            pltpu.VMEM((tokens, HD), bf16),
            pltpu.VMEM((count, HD), bf16),
            pltpu.VMEM((tokens, HD), bf16),
            pltpu.VMEM((count, tokens), bf16),
            pltpu.VMEM((count, HD), jnp.float32),
            pltpu.VMEM((count, HD), bf16),
            pltpu.VMEM((rows, G * heads * HD), bf16),
            pltpu.VMEM(main_mod.shape, bf16),
            pltpu.VMEM(guide_mod.shape, bf16),
            pltpu.VMEM(main_head.shape[::-1], bf16),
            pltpu.VMEM(guide_head.shape[::-1], bf16),
            pltpu.VMEM(latents.shape, jnp.float32),
            dma((5,)), dma((3,)), dma, dma, dma,
        ],
        compiler_params=pltpu.CompilerParams(
            collective_id=0, has_side_effects=True, vmem_limit_bytes=60 * 1024 * 1024
        ),
        cost_estimate=pl.CostEstimate(
            flops=4 * count * tokens * HD, bytes_accessed=4 * tokens * HD * 2,
            transcendentals=count * tokens,
        ),
    )(
        step_index, main_query, main_key, main_value, guide_query, guide_key, guide_value,
        main_mod, guide_mod, main_head.T, guide_head.T, latents,
    )


def solution(mesh):
    return jax.shard_map(
        functools.partial(on_device, mesh.shape["grp"], mesh.shape["seq"]),
        mesh=mesh,
        in_specs=(
            P("seq", "grp", None),
            P("seq", "grp", None),
            P("seq", "grp", None),
            P("seq", None, "grp"),
            P("seq", None, "grp"),
            P("seq", None, "grp"),
            P("seq", "grp", None),
            P(),
            P(),
            P(),
            P(),
            P(),
        ),
        out_specs=(P("seq", "grp", None), P("seq", "grp", None)),
        check_vma=False,
    )
```

time: 38.5 us -> 31.2 us (0.81)
  the two profiles are of different devices: /device:TPU:29 before, /device:TPU:0 now
where the time goes in v3:
time: 31.2 us; the launch traced here: 30.9 us
  Pallas kernels  27.7 us (89%)
  local copies, waits for them, and re-layouts  1.94 us (6%)
  between operations  1.3 us (4%)
    pallas_call x1, Pallas kernels, on_device(): pl.pallas_call(functools.partial(kernel, G, S, R, main_heads, guide_heads...  27.7 us
    unnamed x4, local copies, waits for them, and re-layouts  1.94 us

profile of v3, /device:TPU:0, one launch (start us, length us, event | category | flops | bytes accessed | tf_op | source)
XLA Modules:
  0.0 30.9 jit_solution(3150690924769353394)
XLA Ops:
  1.3 27.7 %shard_map.131 = (f32[1,32,64]{2,1,0:T(8,128)}, f32[1,32,64]{2,1,0:T(8,128)}) custom-call(s32[1]{0:T(128)S(6)} %copy.16.step_ref, bf16[1,32,2560]{2,1,0:T(8,128)(2,1)} %main_q.1, bf16[1,32,2560]{2,1,0:T(8,128)(2,1)} %main_k.1, bf16[1,32,2560]{2,1,0:T(8,128)(2,1)} %main_v.1, bf16[1,128,256]{2,1,0:T(8,128)(2,1)} %guide_q.1, bf16[1,128,256]{2,1,0:T(8,128)(2,1)} %guide_k.1, ...), custom_call_target="tpu_custom_call" | custom-call | flops 536870912 | bytes 1048576 | tf_op jit(solution)/shard_map/pallas_call | solution.py:271
  29.0 0.0 copy-start
  29.0 1.3 %copy.17 = f32[1,32,64]{2,1,0:T(8,128)} copy(f32[1,32,64]{2,1,0:T(8,128)} %get-tuple-element.4) | data formatting | bytes 16384
  30.3 0.0 copy-done
  30.3 0.6 %copy.18 = f32[1,32,64]{2,1,0:T(8,128)} copy(f32[1,32,64]{2,1,0:T(8,128)S(1)} %copy-done) | data formatting | bytes 16384
Async XLA Ops:
  29.0 1.3 %copy-start = (f32[1,32,64]{2,1,0:T(8,128)S(1)}, f32[1,32,64]{2,1,0:T(8,128)}, u32[]{:S(2)}) copy-start(f32[1,32,64]{2,1,0:T(8,128)} %get-tuple-element.5) | copy-start | bytes 24580

commit v4 on v3

--- a/solution.py
+++ b/solution.py
@@ -91,10 +91,6 @@
     part = unit % R
     head_here = slot // 2 + half * (slot % 2)
 
-    def owner(plane, head, r):
-        place = (2 * head) % SLOTS + head // half
-        return (place * R + r + 2 * R * plane) % S
-
     tables = (
         (main_mod, main_table), (guide_mod, guide_table),
         (main_head, main_weight), (guide_head, guide_weight),
@@ -103,67 +99,62 @@
 
     barrier = pltpu.get_barrier_semaphore()
 
-    def greet(i):
-        pl.semaphore_signal(
-            barrier, inc=1,
-            device_id={"grp": (g + (i + 1) // S) % G, "seq": (s + (i + 1) % S) % S},
-        )
-
-    loop(G * S - 1, greet)
+    planes = [lax.rem(g + 1 + d, G) for d in range(G)]
+    for d in range(G):
+        def greet(i, plane=planes[d]):
+            pl.semaphore_signal(
+                barrier, inc=1, device_id={"grp": plane, "seq": lax.rem(s + 1 + i, S)}
+            )
+
+        loop(S if d < G - 1 else S - 1, greet)
     pl.semaphore_wait(barrier, G * S - 1)
 
     main_sources = (main_k.at[0], main_q.at[0], main_v.at[0])
     guide_sources = (guide_k.at[0], guide_q.at[0], guide_v.at[0])
     targets = (keys, queries, values)
-
-    def spread(a, src, dst, plane, head, act):
+    places = (s * block, lax.rem(s, blocks) * block, s * block)
+
+    def unit_of(head):
+        return R * (lax.rem(2 * head, SLOTS) + head // half)
+
+    def send_piece(a, src, dst, plane, first, near):
+        def one(r):
+            seq = lax.rem(first + r, S)
+
+            def away():
+                pltpu.make_async_remote_copy(
+                    src_ref=src, dst_ref=dst, send_sem=send, recv_sem=recv.at[a],
+                    device_id={"grp": plane, "seq": seq},
+                ).start()
+
+            if near:
+                @pl.when(seq == s)
+                def _():
+                    pltpu.make_async_copy(src, dst, recv.at[a]).start()
+
+                pl.when(seq != s)(away)
+            else:
+                away()
+
         if a == QUERY:
-            act(a, src, dst, plane, owner(plane, head, s // blocks))
+            one(s // blocks)
         else:
-            loop(R, lambda r: act(a, src, dst, plane, owner(plane, head, r)))
-
-    def place(a):
-        return (s % blocks) * block if a == QUERY else s * block
-
-    def main_pieces(a, act):
-        number = G * main_heads
-
-        @pl.loop(0, number)
-        def _(i):
-            column = (i + (g + 1) * main_heads + s) % number
-            src = main_sources[a].at[:, pl.ds(aligned(column * HD, HD), HD)]
-            dst = targets[a].at[pl.ds(aligned(place(a) + g * rows, rows), rows), :]
-            spread(a, src, dst, column // main_heads, column % main_heads, act)
-
-    def guide_pieces(a, act):
-        for i in range(guide_heads):
-            head = (i + s) % guide_heads
-            src = guide_sources[a].at[:, pl.ds(aligned(head * HD, HD), HD)]
-            dst = targets[a].at[pl.ds(aligned(place(a), block), block), :]
-            spread(a, src, dst, g, main_heads + head, act)
-
-    def start(a, src, dst, plane, seq):
-        here = (plane == g) & (seq == s)
-
-        @pl.when(here)
-        def _():
-            pltpu.make_async_copy(src, dst, recv.at[a]).start()
-
-        @pl.when(jnp.logical_not(here))
-        def _():
-            pltpu.make_async_remote_copy(
-                src_ref=src, dst_ref=dst, send_sem=send, recv_sem=recv.at[a],
-                device_id={"grp": plane, "seq": seq},
-            ).start()
-
-    def sent(a, src, dst, plane, seq):
-        @pl.when(jnp.logical_not((plane == g) & (seq == s)))
-        def _():
-            wait_for(dst, send)
-
+            loop(R, one)
+
+    turns = [lax.rem(s + i, main_heads) for i in range(main_heads)]
+    offsets = [unit_of(head) for head in turns]
+    shifts = [2 * R * plane for plane in planes]
     for a in range(3):
-        main_pieces(a, start)
-        guide_pieces(a, start)
+        dst = targets[a].at[pl.ds(aligned(places[a] + g * rows, rows), rows), :]
+        for i in range(main_heads):
+            for d in range(G):
+                column = (planes[d] * main_heads + turns[i]) * HD
+                src = main_sources[a].at[:, pl.ds(aligned(column, HD), HD)]
+                send_piece(a, src, dst, planes[d], offsets[i] + shifts[d], d == G - 1)
+        dst = targets[a].at[pl.ds(aligned(places[a], block), block), :]
+        for head in range(guide_heads):
+            src = guide_sources[a].at[:, pl.ds(head * HD, HD)]
+            send_piece(a, src, dst, g, unit_of(main_heads + head) + 2 * R * g, True)
     for i, (src, dst) in enumerate(tables):
         pltpu.make_async_copy(src, dst, table_sem.at[i]).start()
 
@@ -221,9 +212,6 @@
 
                         pl.when(seq != s)(send_out)
 
-    for a in range(3):
-        main_pieces(a, sent)
-        guide_pieces(a, sent)
     for i, (src, dst) in enumerate(tables):
         pltpu.make_async_copy(src, dst, table_sem.at[i]).wait()
     step_now = step_ref[0]
@@ -244,11 +232,33 @@
     velocity[0] = mixed
     advanced[0] = held_latents[0] + (sigma_at(index + 1) - sigma_at(index)) * mixed
 
+    own_part = s // blocks == part
+    is_main = head_here < main_heads
+    is_guide = (head_here >= main_heads) & (head_here < heads)
+
+    def wait_sent(ref, owned):
+        @pl.when(owned)
+        def _():
+            wait_for(ref.at[:, pl.ds(HD, ref.shape[1] - HD)], send)
+
+        @pl.when(jnp.logical_not(owned))
+        def _():
+            wait_for(ref, send)
+
+    for a in range(3):
+        if a != QUERY:
+            for r in range(R - 1):
+                wait_for(main_sources[a], send)
+                wait_for(guide_sources[a], send)
+        mine = own_part if a == QUERY else True
+        wait_sent(main_sources[a], is_main & mine)
+        wait_sent(guide_sources[a], is_guide & mine)
+
     @pl.when(head_here < heads)
     def _():
         wait_for(attended.at[pl.ds(0, count - rows), :], o_send)
 
-        @pl.when(s // blocks != part)
+        @pl.when(jnp.logical_not(own_part))
         def _():
             wait_for(attended.at[pl.ds(0, rows), :], o_send)
 

time: 31.2 us -> 30.7 us (0.984)
  Pallas kernels: 27.7 us -> 27.3 us
    pallas_call x1, Pallas kernels: 27.7 us -> 27.3 us  [on_device(): pl.pallas_call(functools.partial(kernel, G, S, R, main_heads, guide_heads...]
where the time goes in v4:
time: 30.7 us; the launch traced here: 30.6 us
  Pallas kernels  27.3 us (89%)
  local copies, waits for them, and re-layouts  1.94 us (6%)
  between operations  1.3 us (4%)
    pallas_call x1, Pallas kernels, on_device(): pl.pallas_call(functools.partial(kernel, G, S, R, main_heads, guide_heads...  27.3 us
    unnamed x4, local copies, waits for them, and re-layouts  1.94 us

profile of v4, /device:TPU:0, one launch (start us, length us, event | category | flops | bytes accessed | tf_op | source)
XLA Modules:
  0.0 30.6 jit_solution(17746230597813219198)
XLA Ops:
  1.3 27.3 %shard_map.131 = (f32[1,32,64]{2,1,0:T(8,128)}, f32[1,32,64]{2,1,0:T(8,128)}) custom-call(s32[1]{0:T(128)S(6)} %copy.16.step_ref, bf16[1,32,2560]{2,1,0:T(8,128)(2,1)} %main_q.1, bf16[1,32,2560]{2,1,0:T(8,128)(2,1)} %main_k.1, bf16[1,32,2560]{2,1,0:T(8,128)(2,1)} %main_v.1, bf16[1,128,256]{2,1,0:T(8,128)(2,1)} %guide_q.1, bf16[1,128,256]{2,1,0:T(8,128)(2,1)} %guide_k.1, ...), custom_call_target="tpu_custom_call" | custom-call | flops 536870912 | bytes 1048576 | tf_op jit(solution)/shard_map/pallas_call | solution.py:281
  28.6 0.0 copy-start
  28.6 1.3 %copy.17 = f32[1,32,64]{2,1,0:T(8,128)} copy(f32[1,32,64]{2,1,0:T(8,128)} %get-tuple-element.4) | data formatting | bytes 16384
  30.0 0.0 copy-done
  30.0 0.6 %copy.18 = f32[1,32,64]{2,1,0:T(8,128)} copy(f32[1,32,64]{2,1,0:T(8,128)S(1)} %copy-done) | data formatting | bytes 16384
Async XLA Ops:
  28.6 1.3 %copy-start = (f32[1,32,64]{2,1,0:T(8,128)S(1)}, f32[1,32,64]{2,1,0:T(8,128)}, u32[]{:S(2)}) copy-start(f32[1,32,64]{2,1,0:T(8,128)} %get-tuple-element.5) | copy-start | bytes 24580

commit v5 on v4

--- a/solution.py
+++ b/solution.py
@@ -72,7 +72,7 @@
     G, S, R, main_heads, guide_heads,
     step_ref, main_q, main_k, main_v, guide_q, guide_k, guide_v,
     main_mod, guide_mod, main_head, guide_head, latents,
-    velocity, advanced,
+    result,
     keys, queries, values, weights, sums, attended, final,
     main_table, guide_table, main_weight, guide_weight, held_latents,
     table_sem, recv, send, o_recv, o_send,
@@ -123,7 +123,7 @@
 
             def away():
                 pltpu.make_async_remote_copy(
-                    src_ref=src, dst_ref=dst, send_sem=send, recv_sem=recv.at[a],
+                    src_ref=src, dst_ref=dst, send_sem=send.at[a], recv_sem=recv.at[a],
                     device_id={"grp": plane, "seq": seq},
                 ).start()
 
@@ -141,10 +141,34 @@
         else:
             loop(R, one)
 
+    own_part = s // blocks == part
+    is_main = head_here < main_heads
+    is_guide = (head_here >= main_heads) & (head_here < heads)
+
+    def wait_but_own(ref, owned, sem):
+        @pl.when(owned)
+        def _():
+            wait_for(ref.at[:, pl.ds(HD, ref.shape[1] - HD)], sem)
+
+        @pl.when(jnp.logical_not(owned))
+        def _():
+            wait_for(ref, sem)
+
+    def wait_sent(a):
+        if a != QUERY:
+            for r in range(R - 1):
+                wait_for(main_sources[a], send.at[a])
+                wait_for(guide_sources[a], send.at[a])
+        mine = own_part if a == QUERY else True
+        wait_but_own(main_sources[a], is_main & mine, send.at[a])
+        wait_but_own(guide_sources[a], is_guide & mine, send.at[a])
+
     turns = [lax.rem(s + i, main_heads) for i in range(main_heads)]
     offsets = [unit_of(head) for head in turns]
     shifts = [2 * R * plane for plane in planes]
     for a in range(3):
+        if a == VALUE:
+            wait_sent(KEY)
         dst = targets[a].at[pl.ds(aligned(places[a] + g * rows, rows), rows), :]
         for i in range(main_heads):
             for d in range(G):
@@ -229,30 +253,11 @@
     guide_flow = project(taken(main_heads, guide_heads), guide_row, guide_weight)
     mixed = guide_flow + guidance * (main_flow - guide_flow)
     index = jnp.full((1, mixed.shape[1]), step_now, jnp.int32)
-    velocity[0] = mixed
-    advanced[0] = held_latents[0] + (sigma_at(index + 1) - sigma_at(index)) * mixed
-
-    own_part = s // blocks == part
-    is_main = head_here < main_heads
-    is_guide = (head_here >= main_heads) & (head_here < heads)
-
-    def wait_sent(ref, owned):
-        @pl.when(owned)
-        def _():
-            wait_for(ref.at[:, pl.ds(HD, ref.shape[1] - HD)], send)
-
-        @pl.when(jnp.logical_not(owned))
-        def _():
-            wait_for(ref, send)
-
-    for a in range(3):
-        if a != QUERY:
-            for r in range(R - 1):
-                wait_for(main_sources[a], send)
-                wait_for(guide_sources[a], send)
-        mine = own_part if a == QUERY else True
-        wait_sent(main_sources[a], is_main & mine)
-        wait_sent(guide_sources[a], is_guide & mine)
+    result[0] = mixed
+    result[1] = held_latents[0] + (sigma_at(index + 1) - sigma_at(index)) * mixed
+
+    wait_sent(QUERY)
+    wait_sent(VALUE)
 
     @pl.when(head_here < heads)
     def _():
@@ -278,11 +283,11 @@
     anywhere = pl.BlockSpec(memory_space=pltpu.HBM)
     vmem = pl.BlockSpec(memory_space=pltpu.VMEM)
     dma = pltpu.SemaphoreType.DMA
-    return pl.pallas_call(
+    both = pl.pallas_call(
         functools.partial(kernel, G, S, R, main_heads, guide_heads),
-        out_shape=[jax.ShapeDtypeStruct(latents.shape, jnp.float32)] * 2,
+        out_shape=jax.ShapeDtypeStruct((2,) + latents.shape[1:], jnp.float32),
         in_specs=[pl.BlockSpec(memory_space=pltpu.SMEM)] + [anywhere] * 11,
-        out_specs=[vmem, vmem],
+        out_specs=vmem,
         scratch_shapes=[
             pltpu.VMEM((tokens, HD), bf16),
             pltpu.VMEM((count, HD), bf16),
@@ -296,7 +301,7 @@
             pltpu.VMEM(main_head.shape[::-1], bf16),
             pltpu.VMEM(guide_head.shape[::-1], bf16),
             pltpu.VMEM(latents.shape, jnp.float32),
-            dma((5,)), dma((3,)), dma, dma, dma,
+            dma((5,)), dma((3,)), dma((3,)), dma, dma,
         ],
         compiler_params=pltpu.CompilerParams(
             collective_id=0, has_side_effects=True, vmem_limit_bytes=60 * 1024 * 1024
@@ -309,6 +314,7 @@
         step_index, main_query, main_key, main_value, guide_query, guide_key, guide_value,
         main_mod, guide_mod, main_head.T, guide_head.T, latents,
     )
+    return both[:1], both[1:]
 
 
 def solution(mesh):

time: 30.7 us -> 30.3 us (0.987)
  local copies, waits for them, and re-layouts: 1.94 us -> 1.35 us
    unnamed x4 -> x0, local copies, waits for them, and re-layouts: 1.94 us -> none
    slice x0 -> x1, local copies, waits for them, and re-layouts: none -> 1.35 us  [on_device(): return (both[:1], both[1:])]
where the time goes in v5:
time: 30.3 us; the launch traced here: 29.9 us
  Pallas kernels  27.3 us (90%)
  local copies, waits for them, and re-layouts  1.35 us (4%)
  between operations  1.29 us (4%)
    pallas_call x1, Pallas kernels, on_device(): pl.pallas_call(functools.partial(kernel, G, S, R, main_heads, guide_heads...  27.3 us
    slice x1, local copies, waits for them, and re-layouts, on_device(): return (both[:1], both[1:])  1.35 us

profile of v5, /device:TPU:0, one launch (start us, length us, event | category | flops | bytes accessed | tf_op | source)
XLA Modules:
  0.0 29.9 jit_solution(16864481210839389556)
XLA Ops:
  1.3 27.3 %shard_map.131 = f32[2,32,64]{2,1,0:T(8,128)} custom-call(s32[1]{0:T(128)S(6)} %copy.14.step_ref, bf16[1,32,2560]{2,1,0:T(8,128)(2,1)} %main_q.1, bf16[1,32,2560]{2,1,0:T(8,128)(2,1)} %main_k.1, bf16[1,32,2560]{2,1,0:T(8,128)(2,1)} %main_v.1, bf16[1,128,256]{2,1,0:T(8,128)(2,1)} %guide_q.1, bf16[1,128,256]{2,1,0:T(8,128)(2,1)} %guide_k.1, ...), custom_call_target="tpu_custom_call" | custom-call | flops 536870912 | bytes 1048576 | tf_op jit(solution)/shard_map/pallas_call | solution.py:286
  28.6 1.3 %fusion = (f32[1,32,64]{2,1,0:T(8,128)}, f32[1,32,64]{2,1,0:T(8,128)}) fusion(f32[2,32,64]{2,1,0:T(8,128)} %shard_map.131), kind=kLoop, calls=%fused_computation | loop fusion | bytes 32768 | tf_op jit(solution)/shard_map/slice | solution.py:317

commit v6 on v5

--- a/solution.py
+++ b/solution.py
@@ -41,31 +41,41 @@
         pl.loop(0, count)(body)
 
 
-def project(pieces, row, weight_ref):
+def across(left, right):
+    return lax.dot_general(left, right, (((1,), (1,)), ((), ())), preferred_element_type=jnp.float32)
+
+
+def join(product):
+    channels = product.shape[1] // 3
+    return product[:, :channels] + product[:, channels : 2 * channels] + product[:, 2 * channels :]
+
+
+def prepare(row, weight_ref, scaled_ref):
+    weight = weight_ref[...]
+    wide = weight.astype(jnp.float32) * (1.0 + row[1:2].astype(jnp.float32))
+    high = wide.astype(jnp.bfloat16)
+    rest = wide - high.astype(jnp.float32)
+    middle = rest.astype(jnp.bfloat16)
+    low = (rest - middle.astype(jnp.float32)).astype(jnp.bfloat16)
+    scaled_ref[...] = jnp.concatenate([high, middle, low], axis=0)
+    column_sum = join(across(jnp.ones((16, weight.shape[1]), jnp.bfloat16), scaled_ref[...]))
+    shift = across(jnp.broadcast_to(row[0:1].astype(jnp.float32), (16, weight.shape[1])).astype(jnp.bfloat16), weight)
+    return column_sum[0:1], shift[0:1]
+
+
+def project(pieces, scaled_ref, column_sum, shift):
     width = sum(piece.shape[1] for piece in pieces)
+    total = None
+    start = 0
+    for piece in pieces:
+        product = across(piece, scaled_ref[:, start : start + piece.shape[1]])
+        start += piece.shape[1]
+        total = product if total is None else total + product
+    pieces = [piece.astype(jnp.float32) for piece in pieces]
     center = sum(jnp.sum(piece, axis=-1, keepdims=True) for piece in pieces) * (1.0 / width)
     centered = [piece - center for piece in pieces]
     spread = sum(jnp.sum(piece * piece, axis=-1, keepdims=True) for piece in centered) * (1.0 / width)
-    scale = lax.rsqrt(spread + epsilon)
-    total = None
-    start = 0
-    for piece in centered:
-        part = slice(start, start + piece.shape[1])
-        start += piece.shape[1]
-        wide = piece * scale * (1.0 + row[1:2, part]) + row[0:1, part]
-        high = wide.astype(jnp.bfloat16)
-        rest = wide - high.astype(jnp.float32)
-        middle = rest.astype(jnp.bfloat16)
-        low = (rest - middle.astype(jnp.float32)).astype(jnp.bfloat16)
-        product = lax.dot_general(
-            jnp.concatenate([high, middle, low], axis=0),
-            weight_ref[:, part],
-            (((1,), (1,)), ((), ())),
-            preferred_element_type=jnp.float32,
-        )
-        total = product if total is None else total + product
-    rows = total.shape[0] // 3
-    return total[:rows] + total[rows : 2 * rows] + total[2 * rows :]
+    return lax.rsqrt(spread + epsilon) * (join(total) - center * column_sum) + shift
 
 
 def kernel(
@@ -74,7 +84,8 @@
     main_mod, guide_mod, main_head, guide_head, latents,
     result,
     keys, queries, values, weights, sums, attended, final,
-    main_table, guide_table, main_weight, guide_weight, held_latents,
+    main_table, guide_table, main_weight, guide_weight, held_latents, held_step,
+    main_scaled, guide_scaled,
     table_sem, recv, send, o_recv, o_send,
 ):
     g = lax.axis_index("grp")
@@ -94,8 +105,10 @@
     tables = (
         (main_mod, main_table), (guide_mod, guide_table),
         (main_head, main_weight), (guide_head, guide_weight),
-        (latents, held_latents),
+        (latents, held_latents), (step_ref, held_step),
     )
+    for i, (src, dst) in enumerate(tables):
+        pltpu.make_async_copy(src, dst, table_sem.at[i]).start()
 
     barrier = pltpu.get_barrier_semaphore()
 
@@ -180,7 +193,10 @@
             src = guide_sources[a].at[:, pl.ds(head * HD, HD)]
             send_piece(a, src, dst, g, unit_of(main_heads + head) + 2 * R * g, True)
     for i, (src, dst) in enumerate(tables):
-        pltpu.make_async_copy(src, dst, table_sem.at[i]).start()
+        pltpu.make_async_copy(src, dst, table_sem.at[i]).wait()
+    step_now = held_step[0]
+    main_parts = prepare(main_table[step_now], main_weight, main_scaled)
+    guide_parts = prepare(guide_table[step_now], guide_weight, guide_scaled)
 
     factor = math.log2(math.e) / math.sqrt(HD)
     score_rows = max(32, min(256, 256 * 1024 // tokens))
@@ -236,21 +252,16 @@
 
                         pl.when(seq != s)(send_out)
 
-    for i, (src, dst) in enumerate(tables):
-        pltpu.make_async_copy(src, dst, table_sem.at[i]).wait()
-    step_now = step_ref[0]
-    main_row = main_table[step_now].astype(jnp.float32)
-    guide_row = guide_table[step_now].astype(jnp.float32)
     wait_for(final, o_recv)
 
     def taken(first, number):
         return [
-            final[:, (i * heads + first) * HD : (i * heads + first + number) * HD].astype(jnp.float32)
+            final[:, (i * heads + first) * HD : (i * heads + first + number) * HD]
             for i in range(G)
         ]
 
-    main_flow = project(taken(0, main_heads), main_row, main_weight)
-    guide_flow = project(taken(main_heads, guide_heads), guide_row, guide_weight)
+    main_flow = project(taken(0, main_heads), main_scaled, *main_parts)
+    guide_flow = project(taken(main_heads, guide_heads), guide_scaled, *guide_parts)
     mixed = guide_flow + guidance * (main_flow - guide_flow)
     index = jnp.full((1, mixed.shape[1]), step_now, jnp.int32)
     result[0] = mixed
@@ -286,7 +297,7 @@
     both = pl.pallas_call(
         functools.partial(kernel, G, S, R, main_heads, guide_heads),
         out_shape=jax.ShapeDtypeStruct((2,) + latents.shape[1:], jnp.float32),
-        in_specs=[pl.BlockSpec(memory_space=pltpu.SMEM)] + [anywhere] * 11,
+        in_specs=[anywhere] * 12,
         out_specs=vmem,
         scratch_shapes=[
             pltpu.VMEM((tokens, HD), bf16),
@@ -301,7 +312,10 @@
             pltpu.VMEM(main_head.shape[::-1], bf16),
             pltpu.VMEM(guide_head.shape[::-1], bf16),
             pltpu.VMEM(latents.shape, jnp.float32),
-            dma((5,)), dma((3,)), dma((3,)), dma, dma,
+            pltpu.SMEM((1,), jnp.int32),
+            pltpu.VMEM((3 * main_head.shape[1], main_head.shape[0]), bf16),
+            pltpu.VMEM((3 * guide_head.shape[1], guide_head.shape[0]), bf16),
+            dma((6,)), dma((3,)), dma((3,)), dma, dma,
         ],
         compiler_params=pltpu.CompilerParams(
             collective_id=0, has_side_effects=True, vmem_limit_bytes=60 * 1024 * 1024

time: 30.3 us -> 30.4 us (level)
  no operation moved by 1% of the time
where the time goes in v6:
time: 30.4 us; the launch traced here: 30.1 us
  Pallas kernels  27.4 us (90%)
  local copies, waits for them, and re-layouts  1.35 us (4%)
  between operations  1.29 us (4%)
    pallas_call x1, Pallas kernels, on_device(): pl.pallas_call(functools.partial(kernel, G, S, R, main_heads, guide_heads...  27.4 us
    slice x1, local copies, waits for them, and re-layouts, on_device(): return (both[:1], both[1:])  1.35 us

profile of v6, /device:TPU:0, one launch (start us, length us, event | category | flops | bytes accessed | tf_op | source)
XLA Modules:
  0.0 30.1 jit_solution(17239387285533142093)
XLA Ops:
  1.3 27.4 %shard_map.131 = f32[2,32,64]{2,1,0:T(8,128)} custom-call(s32[1]{0:T(128)S(6)} %copy.14.step_ref, bf16[1,32,2560]{2,1,0:T(8,128)(2,1)} %main_q.1, bf16[1,32,2560]{2,1,0:T(8,128)(2,1)} %main_k.1, bf16[1,32,2560]{2,1,0:T(8,128)(2,1)} %main_v.1, bf16[1,128,256]{2,1,0:T(8,128)(2,1)} %guide_q.1, bf16[1,128,256]{2,1,0:T(8,128)(2,1)} %guide_k.1, ...), custom_call_target="tpu_custom_call" | custom-call | flops 536870912 | bytes 1048576 | tf_op jit(solution)/shard_map/pallas_call | solution.py:297
  28.7 1.3 %fusion = (f32[1,32,64]{2,1,0:T(8,128)}, f32[1,32,64]{2,1,0:T(8,128)}) fusion(f32[2,32,64]{2,1,0:T(8,128)} %shard_map.131), kind=kLoop, calls=%fused_computation | loop fusion | bytes 32768 | tf_op jit(solution)/shard_map/slice | solution.py:331

commit v7 on v6

--- a/solution.py
+++ b/solution.py
@@ -85,7 +85,7 @@
     result,
     keys, queries, values, weights, sums, attended, final,
     main_table, guide_table, main_weight, guide_weight, held_latents, held_step,
-    main_scaled, guide_scaled,
+    main_scaled, guide_scaled, scores,
     table_sem, recv, send, o_recv, o_send,
 ):
     g = lax.axis_index("grp")
@@ -200,6 +200,7 @@
 
     factor = math.log2(math.e) / math.sqrt(HD)
     score_rows = max(32, min(256, 256 * 1024 // tokens))
+    strip_rows = max(16, min(32, 32 * 1024 // tokens))
     value_rows = min(256, count)
     value_blocks = count // value_rows
 
@@ -209,17 +210,17 @@
         wait_for(queries, recv.at[QUERY])
 
         def score(i):
-            at = pl.ds(i * score_rows, score_rows)
-            scores = lax.dot_general(
-                queries[at, :], keys[...], (((1,), (1,)), ((), ())),
-                preferred_element_type=jnp.float32,
-            )
-            highest = jnp.max(scores, axis=-1, keepdims=True)
-            unrounded = jnp.exp2((scores - highest) * factor)
-            sums[at, :] = jnp.broadcast_to(
-                jnp.sum(unrounded, axis=-1, keepdims=True), (score_rows, HD)
-            )
-            weights[at, :] = unrounded.astype(jnp.bfloat16)
+            held = scores.at[i % 2]
+            held[...] = across(queries[pl.ds(i * score_rows, score_rows), :], keys[...])
+            for j in range(score_rows // strip_rows):
+                strip = held[pl.ds(j * strip_rows, strip_rows), :]
+                highest = jnp.max(strip, axis=-1, keepdims=True)
+                unrounded = jnp.exp2((strip - highest) * factor)
+                at = pl.ds(i * score_rows + j * strip_rows, strip_rows)
+                sums[at, :] = jnp.broadcast_to(
+                    jnp.sum(unrounded, axis=-1, keepdims=True), (strip_rows, HD)
+                )
+                weights[at, :] = unrounded.astype(jnp.bfloat16)
 
         loop(count // score_rows, score)
         wait_for(values, recv.at[VALUE])
@@ -315,6 +316,7 @@
             pltpu.SMEM((1,), jnp.int32),
             pltpu.VMEM((3 * main_head.shape[1], main_head.shape[0]), bf16),
             pltpu.VMEM((3 * guide_head.shape[1], guide_head.shape[0]), bf16),
+            pltpu.VMEM((2, max(32, min(256, 256 * 1024 // tokens)), tokens), jnp.float32),
             dma((6,)), dma((3,)), dma((3,)), dma, dma,
         ],
         compiler_params=pltpu.CompilerParams(

time: 30.4 us -> 30.4 us (level)
  no operation moved by 1% of the time
where the time goes in v7:
time: 30.4 us; the launch traced here: 30.1 us
  Pallas kernels  27.4 us (90%)
  local copies, waits for them, and re-layouts  1.35 us (4%)
  between operations  1.29 us (4%)
    pallas_call x1, Pallas kernels, on_device(): pl.pallas_call(functools.partial(kernel, G, S, R, main_heads, guide_heads...  27.4 us
    slice x1, local copies, waits for them, and re-layouts, on_device(): return (both[:1], both[1:])  1.35 us

profile of v7, /device:TPU:0, one launch (start us, length us, event | category | flops | bytes accessed | tf_op | source)
XLA Modules:
  0.0 30.1 jit_solution(5649500289427964701)
XLA Ops:
  1.3 27.4 %shard_map.131 = f32[2,32,64]{2,1,0:T(8,128)} custom-call(s32[1]{0:T(128)S(6)} %copy.14.step_ref, bf16[1,32,2560]{2,1,0:T(8,128)(2,1)} %main_q.1, bf16[1,32,2560]{2,1,0:T(8,128)(2,1)} %main_k.1, bf16[1,32,2560]{2,1,0:T(8,128)(2,1)} %main_v.1, bf16[1,128,256]{2,1,0:T(8,128)(2,1)} %guide_q.1, bf16[1,128,256]{2,1,0:T(8,128)(2,1)} %guide_k.1, ...), custom_call_target="tpu_custom_call" | custom-call | flops 536870912 | bytes 1048576 | tf_op jit(solution)/shard_map/pallas_call | solution.py:298
  28.7 1.3 %fusion = (f32[1,32,64]{2,1,0:T(8,128)}, f32[1,32,64]{2,1,0:T(8,128)}) fusion(f32[2,32,64]{2,1,0:T(8,128)} %shard_map.131), kind=kLoop, calls=%fused_computation | loop fusion | bytes 32768 | tf_op jit(solution)/shard_map/slice | solution.py:333

commit v8 on v5

--- a/solution.py
+++ b/solution.py
@@ -75,7 +75,7 @@
     result,
     keys, queries, values, weights, sums, attended, final,
     main_table, guide_table, main_weight, guide_weight, held_latents,
-    table_sem, recv, send, o_recv, o_send,
+    main_held, guide_held, in_sem, table_sem, recv, send, o_recv, o_send,
 ):
     g = lax.axis_index("grp")
     s = lax.axis_index("seq")
@@ -97,6 +97,16 @@
         (latents, held_latents),
     )
 
+    inputs = (main_k, main_q, main_v, guide_k, guide_q, guide_v)
+    staged = [main_held.at[a] for a in range(3)] + [guide_held.at[a] for a in range(3)]
+    arrivals = [
+        pltpu.make_async_copy(src.at[0], dst, in_sem.at[i])
+        for i, (src, dst) in enumerate(zip(inputs, staged))
+    ]
+    for a in range(3):
+        arrivals[a].start()
+        arrivals[3 + a].start()
+
     barrier = pltpu.get_barrier_semaphore()
 
     planes = [lax.rem(g + 1 + d, G) for d in range(G)]
@@ -109,8 +119,8 @@
         loop(S if d < G - 1 else S - 1, greet)
     pl.semaphore_wait(barrier, G * S - 1)
 
-    main_sources = (main_k.at[0], main_q.at[0], main_v.at[0])
-    guide_sources = (guide_k.at[0], guide_q.at[0], guide_v.at[0])
+    main_sources = staged[:3]
+    guide_sources = staged[3:]
     targets = (keys, queries, values)
     places = (s * block, lax.rem(s, blocks) * block, s * block)
 
@@ -169,6 +179,8 @@
     for a in range(3):
         if a == VALUE:
             wait_sent(KEY)
+        arrivals[a].wait()
+        arrivals[3 + a].wait()
         dst = targets[a].at[pl.ds(aligned(places[a] + g * rows, rows), rows), :]
         for i in range(main_heads):
             for d in range(G):
@@ -301,7 +313,9 @@
             pltpu.VMEM(main_head.shape[::-1], bf16),
             pltpu.VMEM(guide_head.shape[::-1], bf16),
             pltpu.VMEM(latents.shape, jnp.float32),
-            dma((5,)), dma((3,)), dma((3,)), dma, dma,
+            pltpu.VMEM((3,) + main_query.shape[1:], bf16),
+            pltpu.VMEM((3,) + guide_query.shape[1:], bf16),
+            dma((6,)), dma((5,)), dma((3,)), dma((3,)), dma, dma,
         ],
         compiler_params=pltpu.CompilerParams(
             collective_id=0, has_side_effects=True, vmem_limit_bytes=60 * 1024 * 1024

time: 30.3 us -> 30.1 us (level)
  no operation moved by 1% of the time
where the time goes in v8:
time: 30.1 us; the launch traced here: 29.8 us
  Pallas kernels  27.2 us (90%)
  local copies, waits for them, and re-layouts  1.35 us (4%)
  between operations  1.29 us (4%)
    pallas_call x1, Pallas kernels, on_device(): pl.pallas_call(functools.partial(kernel, G, S, R, main_heads, guide_heads...  27.2 us
    slice x1, local copies, waits for them, and re-layouts, on_device(): return (both[:1], both[1:])  1.35 us

profile of v8, /device:TPU:0, one launch (start us, length us, event | category | flops | bytes accessed | tf_op | source)
XLA Modules:
  0.0 29.8 jit_solution(11195129953566105280)
XLA Ops:
  1.3 27.2 %shard_map.131 = f32[2,32,64]{2,1,0:T(8,128)} custom-call(s32[1]{0:T(128)S(6)} %copy.14.step_ref, bf16[1,32,2560]{2,1,0:T(8,128)(2,1)} %main_q.1, bf16[1,32,2560]{2,1,0:T(8,128)(2,1)} %main_k.1, bf16[1,32,2560]{2,1,0:T(8,128)(2,1)} %main_v.1, bf16[1,128,256]{2,1,0:T(8,128)(2,1)} %guide_q.1, bf16[1,128,256]{2,1,0:T(8,128)(2,1)} %guide_k.1, ...), custom_call_target="tpu_custom_call" | custom-call | flops 536870912 | bytes 1048576 | tf_op jit(solution)/shard_map/pallas_call | solution.py:298
  28.5 1.3 %fusion = (f32[1,32,64]{2,1,0:T(8,128)}, f32[1,32,64]{2,1,0:T(8,128)}) fusion(f32[2,32,64]{2,1,0:T(8,128)} %shard_map.131), kind=kLoop, calls=%fused_computation | loop fusion | bytes 32768 | tf_op jit(solution)/shard_map/slice | solution.py:331
